TPU v7x, 128 devices: a whole 4x4x4 slice. The times are simulated.
128 devices in a mesh: tseg: 2 (over y_lo), inp: 64 (over x, z, y_hi, core).
Axes of the slice: x: 4, y: 4 (y_hi: 2, y_lo: 2; y = y_hi * 2 + y_lo), z: 4, core: 2. Of those that a mesh axis runs over, the one named last changes fastest.
Arguments:
- samples: bfloat16 [512, 524288], P('inp', 'tseg')
- delays: int32 [512], P('inp'), may hold values from 0 to 8192, as said below
- flags: int32 [512], P('inp'), may hold values 0 or 1
- taps: float32 [16, 1024], replicated, may hold values from -1.5 to 1.5
Outputs:
- vis_real: float32 [512, 512, 512], P(('tseg', 'inp'))
- vis_imag: float32 [512, 512, 512], P(('tseg', 'inp'))
Inputs may be any that keep to these rules, and one draw needn't show every extreme that they name: `delays`: some input has delay 0 and some input has delay 8192.
All inputs are finite; a program needn't handle non-finite values. No bound on the sum of `flags` on one device may be relied on, other than what follows from the above.
Results may differ from a plain program's by a relative error of at most 0.0075.
Values may be sent and summed in bfloat16 or wider, within the bound.
A program may use at most 64 MiB of HBM per device.

v0:
```python
import functools
import math

import jax
import jax.numpy as jnp
import ml_dtypes
import numpy as np
from jax import lax
from jax.experimental import pallas as pl
from jax.experimental.pallas import tpu as pltpu
from jax.sharding import PartitionSpec as P

MESH = pl.DeviceIdType.MESH
TAPS = 16
FRAME = 1024
HALO = 23552
LANES = 128
BLOCKS = FRAME // LANES
HERE = 8
S_DEV = 256
HALF = 128
CHAN = 4
ROWS = CHAN * 2 * HERE
FIRST = HALO // FRAME + 1
RUN = FIRST + S_DEV + 1
WINDOW = HALF + TAPS
SPLIT = 103
O_STRIDE = HERE + 1
PIECES = ((103, 40), (143, 40), (183, 40), (223, 33))
GREET_FIRST = 37
GREET_STEP = 3
AT_ONCE = 5
SHAPES = {64: (4, 4, 2), 4: (2, 1, 1)}


def dft_rows(nx, ny, nz):
    count = nx * ny * nz * 2
    inp = count // 2
    k = np.arange(FRAME)[None, :]
    q = np.arange(count * CHAN)[:, None]
    phase = ((q * k) % FRAME).astype(np.float64) * (2.0 * math.pi / FRAME)
    parts = np.stack([np.cos(phase), -np.sin(phase)], axis=1) / math.sqrt(FRAME)
    parts = parts.astype(np.float32).astype(ml_dtypes.bfloat16)
    parts = parts.reshape(2, nx, nz, ny // 2, 2, CHAN * 2, FRAME)
    parts = parts.transpose(1, 3, 0, 2, 4, 5, 6)
    assert inp * 2 == count
    return parts.reshape(nx * ny * nz, 2 * CHAN * 2, FRAME)


def rem(a, b):
    return lax.rem(a, jnp.int32(b))


def div(a, b):
    return lax.div(a, jnp.int32(b))


class Work:
    def __init__(self, dims, delays, flags, refs):
        self.dims = dims
        self.delays, self.flags = delays, flags
        self.rows_table, self.runs, self.tap_rows, self.delayed, self.frames, self.turned = refs
        nx, ny, nz = dims
        self.inp = nx * nz * ny
        self.tseg = lax.axis_index("tseg")
        self.here = lax.axis_index("inp")
        self.me = self.tseg * self.inp + self.here
        self.my_core = rem(self.here, 2)
        self.my_y = rem(div(self.here, 2), ny // 2) * 2 + self.tseg
        self.my_z = rem(div(self.here, ny), nz)
        self.my_x = div(self.here, ny * nz)
        self.sign = 1 - 2 * self.my_core
        self.lane = lax.broadcasted_iota(jnp.int32, (HERE, LANES), 1)

    def chip_of(self, group, step):
        nx, ny, nz = self.dims
        dx = rem(step, nx)
        dy = div(step, nx)
        dz = group + 2 * nz - dx - dy
        return (
            rem(self.my_x + nx + self.sign * dx, nx),
            rem(self.my_y + ny + self.sign * dy, ny),
            rem(self.my_z + 4 * nz + self.sign * dz, nz),
        )

    def device(self, chip, core):
        nx, ny, nz = self.dims
        x, y, z = chip
        return rem(y, 2), ((x * nz + z) * (ny // 2) + div(y, 2)) * 2 + core

    def place_taps(self, taps):
        for block in range(BLOCKS):
            for p in range(TAPS):
                self.tap_rows[pl.ds((block * TAPS + p) * 8, 8), :] = jnp.broadcast_to(
                    taps[p : p + 1, block * LANES : (block + 1) * LANES], (8, LANES)
                )

    def spread(self, source, first, frame_range, unroll, each=None):
        row = lax.broadcasted_iota(jnp.int32, (HERE, LANES), 0)
        turn = jnp.zeros((HERE, LANES), jnp.int32)
        for i in range(HERE):
            turn = jnp.where(row == i, self.delays[i] % LANES, turn)
        index = (self.lane - turn + LANES) % LANES

        @pl.loop(*frame_range, step=unroll)
        def _(start):
            for frame in range(unroll):
                frame = start + frame
                values = source[:, pl.ds(pl.multiple_of(frame * FRAME, FRAME), FRAME)].astype(
                    jnp.float32
                )
                for block in range(BLOCKS):
                    moved = jnp.take_along_axis(
                        values[:, block * LANES : (block + 1) * LANES], index, axis=1
                    )
                    self.runs[pl.ds(block * HERE * RUN + first + frame, HERE, stride=RUN), :] = (
                        moved
                    )
            if each is not None:
                each(div(start - frame_range[0], unroll))

    def run_half(self, half, each=None):
        base = half * HALF - (TAPS - 1)

        @pl.loop(0, HERE * BLOCKS)
        def _(run):
            i = div(run, BLOCKS)
            block = rem(run, BLOCKS)
            delay = self.delays[i]
            keep = self.lane >= delay % LANES
            weight = self.flags[i].astype(jnp.float32)

            def start(back):
                moved = block - delay // LANES - back + 9 * BLOCKS
                return (moved % BLOCKS * HERE + i) * RUN + moved // BLOCKS - 9 + FIRST + base

            now, before = start(0), start(1)
            for f in range(0, WINDOW, 8):
                self.delayed[pl.ds(pl.multiple_of(run * WINDOW, 8) + f, 8), :] = jnp.where(
                    keep, self.runs[pl.ds(now + f, 8), :], self.runs[pl.ds(before + f, 8), :]
                )
            tap = [self.tap_rows[pl.ds((block * TAPS + p) * 8, 8), :] for p in range(TAPS)]
            total = {}
            for f in range(HALF + 8):
                values = self.delayed[pl.ds(run * WINDOW + f, 8), :]
                for p in (f % 8 + 8, f % 8):
                    s = f - p
                    if 0 <= s < HALF:
                        total[s] = tap[p] * values if p == 0 else total[s] + tap[p] * values
                if f % 16 == 15 and f > 16:
                    pair = [total.pop(f - 31), total.pop(f - 23)]
                    self.frames[
                        pl.ds(pl.multiple_of(i * HALF, HALF) + f - 31, 16),
                        pl.ds(pl.multiple_of(block * LANES, LANES), LANES),
                    ] = (jnp.concatenate(pair, axis=0) * weight).astype(jnp.bfloat16)
            pair = [total.pop(HALF - 16), total.pop(HALF - 8)]
            self.frames[
                pl.ds(pl.multiple_of(i * HALF, HALF) + HALF - 16, 16),
                pl.ds(pl.multiple_of(block * LANES, LANES), LANES),
            ] = (jnp.concatenate(pair, axis=0) * weight).astype(jnp.bfloat16)
            assert not total
            if each is not None:
                each(run)

    def transform(self, group):
        nx, ny, nz = self.dims
        per_group = nx * ny
        chips = [self.chip_of(group, jnp.int32(step)) for step in range(per_group)]
        rows = jnp.concatenate(
            [self.rows_table[(x * ny + y) * nz + z] for x, y, z in chips], axis=0
        )

        for pair in range(HERE // 2):
            values = self.frames[pair * 2 * HALF : (pair + 1) * 2 * HALF, :]
            spectra = lax.dot_general(
                rows, values, (((1,), (1,)), ((), ())), preferred_element_type=jnp.float32
            )
            for dest in range(2 * per_group):
                for j in range(2):
                    self.turned[
                        pl.ds(dest * 8 * O_STRIDE + pair * 2 + j, 8, stride=O_STRIDE), :
                    ] = spectra[dest * 8 : (dest + 1) * 8, j * HALF : (j + 1) * HALF]

    def pack(self, dest, target):
        for m in range(0, 8, 2):
            pair_rows = jnp.concatenate(
                [
                    self.turned[pl.ds((dest * 8 + m) * O_STRIDE, HERE), :],
                    self.turned[pl.ds((dest * 8 + m + 1) * O_STRIDE, HERE), :],
                ],
                axis=0,
            )
            target[m * 8 : (m + 2) * 8, :] = pair_rows.astype(jnp.bfloat16)

    def send(self, source, target, device, send_sem, recv_sem):
        pltpu.make_async_remote_copy(
            src_ref=source,
            dst_ref=target,
            send_sem=send_sem,
            recv_sem=recv_sem,
            device_id=device,
            device_id_type=MESH,
        ).start()

    def send_direct(self, group, step, change, source, target, send_sem, recv_sem):
        core = self.my_core if change == 0 else 1 - self.my_core
        slot = (group * self.dims[0] * self.dims[1] + step) * 2 + core
        chip = self.chip_of(group, step)
        self.send(
            source.at[slot], target.at[self.me], self.device(chip, core), send_sem, recv_sem
        )


def exchange_kernel(dims, samples, delays, flags, taps, table, out, raw, rim, ready, *rest):
    refs, sems = rest[:6], rest[6:]
    load_sem, table_sem, rim_send, rim_recv, send_sem, recv_sem, own_sem = sems
    work = Work(dims, delays, flags, refs)
    nx, ny, nz = dims
    per_group = nx * ny
    inp = nx * ny * nz
    devices = 2 * inp

    def load(first, count, sem):
        part = pl.ds(first * FRAME, count * FRAME)
        copy = pltpu.make_async_copy(samples.at[:, part], raw.at[:, part], sem)
        copy.start()
        return copy

    late_loads = [
        load(first, count, load_sem.at[piece]) for piece, (first, count) in enumerate(PIECES)
    ]
    fetch = pltpu.make_async_copy(table, work.rows_table, table_sem)
    fetch.start()
    early_load = load(0, SPLIT, load_sem.at[len(PIECES)])
    barrier = pltpu.get_barrier_semaphore()

    def greet(step):
        other = rem(work.me + step, devices)
        pl.semaphore_signal(
            barrier, inc=1, device_id=(div(other, inp), rem(other, inp)), device_id_type=MESH
        )

    @pl.loop(1, 1 + GREET_FIRST)
    def _(step):
        greet(step)

    work.place_taps(taps)

    def send_direct(half, group, step):
        common = (ready.at[half], out.at[half], send_sem.at[half], recv_sem.at[half])

        @pl.when(group + step > 0)
        def _():
            work.send_direct(group, step, 0, *common)

        @pl.when(group + step == 0)
        def _():
            pltpu.make_async_copy(
                ready.at[half, work.my_core], out.at[half, work.me], own_sem.at[half]
            ).start()

        work.send_direct(group, step, 1, *common)

    def send_chip(half, slot):
        send_direct(half, div(slot, per_group), rem(slot, per_group))

    def send_later(order):
        later = per_group - AT_ONCE
        send_direct(1, div(order, later), AT_ONCE + rem(order, later))

    def transform_half(half, each_group, each_step):
        @pl.loop(0, nz)
        def _(group):
            work.transform(group)

            @pl.loop(0, per_group, step=4)
            def _(chips):
                for dest in range(8):
                    dest = chips * 2 + dest
                    work.pack(dest, ready.at[half, group * 2 * per_group + dest])
                if each_step is not None:
                    each_step(group * 4 + div(chips, 4))

            if each_group is not None:
                each_group(group)

    def some_now(group):
        @pl.loop(0, AT_ONCE)
        def _(step):
            send_direct(1, group, step)

    def in_spread(step):
        @pl.when(rem(step, 3) == 0)
        def _():
            send_later(div(step, 3))

    def in_filter(run):
        @pl.when(rem(run, 3) == 0)
        def _():
            send_later(9 + div(run, 3))

    def in_transform(step):
        @pl.when(step < 13)
        def _():
            send_later(31 + step)

    greeted = 1 + GREET_FIRST
    for piece, (first, count) in enumerate(PIECES):
        late_loads[piece].wait()
        whole = count // 4 * 4

        def in_late(step, begin=greeted):
            for k in range(GREET_STEP):
                greet(begin + step * GREET_STEP + k)

        greeting = greeted < devices
        work.spread(raw, FIRST, (first, first + whole), 4, in_late if greeting else None)
        if greeting:
            greeted += whole // 4 * GREET_STEP
        if whole < count:
            work.spread(raw, FIRST, (first + whole, first + count), 1)
    assert greeted == devices
    pl.semaphore_wait(barrier, devices - 1)
    rim_copy = pltpu.make_async_remote_copy(
        src_ref=samples.at[:, pl.ds(S_DEV * FRAME - HALO, HALO)],
        dst_ref=rim,
        send_sem=rim_send,
        recv_sem=rim_recv,
        device_id=(1 - work.tseg, work.here),
        device_id_type=MESH,
    )
    rim_copy.start()
    work.run_half(1)
    fetch.wait()
    transform_half(1, some_now, None)

    early_load.wait()
    work.spread(raw, FIRST, (0, SPLIT - 3), 4, in_spread)
    work.spread(raw, FIRST, (SPLIT - 3, SPLIT), 1)
    rim_copy.wait()

    @pl.when(work.tseg == 0)
    def _():
        rim[...] = jnp.zeros_like(rim)

    work.spread(rim, 1, (0, 20), 4)
    work.spread(rim, 1, (20, HALO // FRAME), 1)
    work.run_half(0, in_filter)
    transform_half(0, None, in_transform)

    @pl.loop(0, nz * per_group)
    def _(slot):
        send_chip(0, slot)

    for half in (1, 0):
        pltpu.make_async_copy(
            ready.at[half, work.my_core], out.at[half, work.me], own_sem.at[half]
        ).wait()
        sent = ready.at[half, pl.ds(0, devices - 1)]
        pltpu.make_async_copy(sent, sent, send_sem.at[half]).wait()
        arrived = out.at[half, pl.ds(0, devices - 1)]
        pltpu.make_async_copy(arrived, arrived, recv_sem.at[half]).wait()


def correlate_kernel(segments, scale, source, vis_real, vis_imag, loaded, sem):
    channel = pl.program_id(0)

    def load(c, half):
        rows = pl.ds(pl.multiple_of(c * 2 * HERE, 2 * HERE), 2 * HERE)
        return pltpu.make_async_copy(
            source.at[half, :, rows, :], loaded.at[c, half], sem.at[c, half]
        )

    @pl.when(channel == 0)
    def _():
        for c in range(CHAN):
            for half in range(2):
                load(c, half).start()

    for half in range(2):
        load(channel, half).wait()
    spectra = loaded.at[channel]
    sources = spectra.shape[1] // segments
    inputs = sources * HERE
    real, imag = [], []
    for half in range(2):
        for segment in range(segments):
            piece = spectra[half, segment * sources : (segment + 1) * sources].astype(jnp.float32)
            real.append(piece[:, :HERE].reshape(inputs, HALF).astype(jnp.bfloat16))
            imag.append(piece[:, HERE:].reshape(inputs, HALF).astype(jnp.bfloat16))
    real = jnp.concatenate(real, axis=1)
    imag = jnp.concatenate(imag, axis=1)

    def product(a, b):
        return lax.dot_general(a, b, (((1,), (1,)), ((), ())), preferred_element_type=jnp.float32)

    middle = inputs // 2
    low, high = slice(0, middle), slice(middle, inputs)
    for rows, columns in ((low, low), (high, high), (low, high)):
        block = product(real[rows], real[columns]) + product(imag[rows], imag[columns])
        vis_real[0, rows, columns] = block * scale
        if rows != columns:
            vis_real[0, columns, rows] = block.T * scale
    cross = product(real, imag)
    vis_imag[0] = (cross - cross.T) * scale


def per_device(samples, delays, flags, taps, *, segments, inp):
    nx, nz, ny_hi = SHAPES[inp]
    dims = (nx, 2 * ny_hi, nz)
    devices = segments * inp
    per_group = nx * 2 * ny_hi
    table = jnp.asarray(dft_rows(*dims))
    anywhere = pl.BlockSpec(memory_space=pl.ANY)
    in_specs = [
        anywhere,
        pl.BlockSpec(memory_space=pltpu.SMEM),
        pl.BlockSpec(memory_space=pltpu.SMEM),
        pl.BlockSpec(memory_space=pltpu.VMEM),
        anywhere,
    ]
    work_scratch = [
        pltpu.VMEM((nz * per_group, 16, FRAME), jnp.bfloat16),
        pltpu.VMEM((BLOCKS * HERE * RUN + 8, LANES), jnp.float32),
        pltpu.VMEM((BLOCKS * TAPS * 8, LANES), jnp.float32),
        pltpu.VMEM((HERE * BLOCKS * WINDOW, LANES), jnp.float32),
        pltpu.VMEM((HERE * HALF, FRAME), jnp.bfloat16),
        pltpu.VMEM((2 * per_group * 8 * O_STRIDE, LANES), jnp.float32),
    ]
    raw = pltpu.VMEM((HERE, S_DEV * FRAME), jnp.bfloat16)
    dma = pltpu.SemaphoreType.DMA
    spectra = pl.pallas_call(
        functools.partial(exchange_kernel, dims),
        out_shape=jax.ShapeDtypeStruct((2, devices, ROWS, HALF), jnp.bfloat16),
        in_specs=in_specs,
        out_specs=anywhere,
        scratch_shapes=[
            raw,
            pltpu.VMEM((HERE, HALO), jnp.bfloat16),
            pltpu.VMEM((2, devices, ROWS, HALF), jnp.bfloat16),
            *work_scratch,
            dma((len(PIECES) + 1,)),
            *[dma] * 3,
            *[dma((2,))] * 3,
        ],
        compiler_params=pltpu.CompilerParams(
            collective_id=0, has_side_effects=True, vmem_limit_bytes=60 * 2**20
        ),
        name="exchange",
    )(samples, delays, flags, taps, table)
    inputs = inp * HERE
    visibility = jax.ShapeDtypeStruct((CHAN, inputs, inputs), jnp.float32)
    return pl.pallas_call(
        functools.partial(correlate_kernel, segments, 1.0 / (S_DEV * segments)),
        out_shape=(visibility, visibility),
        grid=(CHAN,),
        in_specs=[anywhere],
        out_specs=(
            pl.BlockSpec((1, inputs, inputs), lambda c: (c, 0, 0)),
            pl.BlockSpec((1, inputs, inputs), lambda c: (c, 0, 0)),
        ),
        scratch_shapes=[
            pltpu.VMEM((CHAN, 2, devices, 2 * HERE, HALF), jnp.bfloat16),
            dma((CHAN, 2)),
        ],
        compiler_params=pltpu.CompilerParams(vmem_limit_bytes=60 * 2**20),
        name="correlate",
    )(spectra)


def solution(mesh):
    segments, inp = mesh.shape["tseg"], mesh.shape["inp"]
    return jax.shard_map(
        functools.partial(per_device, segments=segments, inp=inp),
        mesh=mesh,
        in_specs=(P("inp", "tseg"), P("inp"), P("inp"), P()),
        out_specs=(P(("tseg", "inp"), None, None), P(("tseg", "inp"), None, None)),
        check_vma=False,
    )
```

profile of v0, /device:TPU:1, one launch (start us, length us, event | category | flops | bytes accessed | tf_op | source)
XLA Modules:
  0.0 80.7 jit_solution(8401164164647366652)
XLA Ops:
  0.6 73.4 %exchange.1.source = bf16[2,128,64,128]{3,2,1,0:T(8,128)(2,1)} custom-call(bf16[8,262144]{1,0:T(8,128)(2,1)} %samples.1, s32[8]{0:T(128)} %delays.1, s32[8]{0:T(128)} %flags.1, f32[16,1024]{1,0:T(8,128)} %taps.1, bf16[64,16,1024]{2,1,0:T(8,128)(2,1)} %constant.2.clone.table), custom_call_target="tpu_custom_call" | custom-call | tf_op jit(solution)/shard_map/exchange/pallas_call | solution.py:432
  74.1 6.6 %correlate.1 = (f32[4,512,512]{2,1,0:T(8,128)}, f32[4,512,512]{2,1,0:T(8,128)}) custom-call(bf16[2,128,64,128]{3,2,1,0:T(8,128)(2,1)} %exchange.1.source), custom_call_target="tpu_custom_call" | custom-call | tf_op jit(solution)/shard_map/correlate/pallas_call | solution.py:453
where the time goes:
time: 80.9 us; the launch traced here: 80.7 us
  Pallas kernels  80.1 us (99%)
    pallas_call x1, Pallas kernels, per_device(): pl.pallas_call(functools.partial(exchange_kernel, dims), out_shape=jax.Sh...  73.4 us
    pallas_call x1, Pallas kernels, per_device(): pl.pallas_call(functools.partial(correlate_kernel, segments, 1.0 / (S_DEV...  6.62 us

commit v1 on v0

--- a/solution.py
+++ b/solution.py
@@ -29,7 +29,8 @@
 PIECES = ((103, 40), (143, 40), (183, 40), (223, 33))
 GREET_FIRST = 37
 GREET_STEP = 3
-AT_ONCE = 5
+PART = ROWS // 2
+AT_ONCE = 8
 SHAPES = {64: (4, 4, 2), 4: (2, 1, 1)}
 
 
@@ -119,10 +120,10 @@
             if each is not None:
                 each(div(start - frame_range[0], unroll))
 
-    def run_half(self, half, each=None):
+    def run_half(self, half, inputs, each=None):
         base = half * HALF - (TAPS - 1)
 
-        @pl.loop(0, HERE * BLOCKS)
+        @pl.loop(inputs[0] * BLOCKS, inputs[1] * BLOCKS)
         def _(run):
             i = div(run, BLOCKS)
             block = rem(run, BLOCKS)
@@ -162,7 +163,7 @@
             if each is not None:
                 each(run)
 
-    def transform(self, group):
+    def transform(self, group, inputs, stride):
         nx, ny, nz = self.dims
         per_group = nx * ny
         chips = [self.chip_of(group, jnp.int32(step)) for step in range(per_group)]
@@ -170,15 +171,15 @@
             [self.rows_table[(x * ny + y) * nz + z] for x, y, z in chips], axis=0
         )
 
-        for pair in range(HERE // 2):
-            values = self.frames[pair * 2 * HALF : (pair + 1) * 2 * HALF, :]
+        for first in range(*inputs, 2):
+            values = self.frames[first * HALF : (first + 2) * HALF, :]
             spectra = lax.dot_general(
                 rows, values, (((1,), (1,)), ((), ())), preferred_element_type=jnp.float32
             )
             for dest in range(2 * per_group):
                 for j in range(2):
                     self.turned[
-                        pl.ds(dest * 8 * O_STRIDE + pair * 2 + j, 8, stride=O_STRIDE), :
+                        pl.ds(dest * 8 * stride + first - inputs[0] + j, 8, stride=stride), :
                     ] = spectra[dest * 8 : (dest + 1) * 8, j * HALF : (j + 1) * HALF]
 
     def pack(self, dest, target):
@@ -192,6 +193,10 @@
             )
             target[m * 8 : (m + 2) * 8, :] = pair_rows.astype(jnp.bfloat16)
 
+    def pack_part(self, dest, target, part):
+        rows = self.turned[pl.ds(pl.multiple_of(dest * PART, PART), PART), :]
+        target[part * PART : (part + 1) * PART, :] = rows.astype(jnp.bfloat16)
+
     def send(self, source, target, device, send_sem, recv_sem):
         pltpu.make_async_remote_copy(
             src_ref=source,
@@ -202,12 +207,16 @@
             device_id_type=MESH,
         ).start()
 
-    def send_direct(self, group, step, change, source, target, send_sem, recv_sem):
+    def send_direct(self, group, step, change, rows, source, target, send_sem, recv_sem):
         core = self.my_core if change == 0 else 1 - self.my_core
         slot = (group * self.dims[0] * self.dims[1] + step) * 2 + core
         chip = self.chip_of(group, step)
         self.send(
-            source.at[slot], target.at[self.me], self.device(chip, core), send_sem, recv_sem
+            source.at[slot, rows],
+            target.at[self.me, rows],
+            self.device(chip, core),
+            send_sem,
+            recv_sem,
         )
 
 
@@ -246,8 +255,9 @@
 
     work.place_taps(taps)
 
-    def send_direct(half, group, step):
-        common = (ready.at[half], out.at[half], send_sem.at[half], recv_sem.at[half])
+    def send_chip(half, group, step, part=None):
+        rows = pl.ds(0, ROWS) if part is None else pl.ds(part * PART, PART)
+        common = (rows, ready.at[half], out.at[half], send_sem.at[half], recv_sem.at[half])
 
         @pl.when(group + step > 0)
         def _():
@@ -256,53 +266,54 @@
         @pl.when(group + step == 0)
         def _():
             pltpu.make_async_copy(
-                ready.at[half, work.my_core], out.at[half, work.me], own_sem.at[half]
+                ready.at[half, work.my_core, rows], out.at[half, work.me, rows], own_sem.at[half]
             ).start()
 
         work.send_direct(group, step, 1, *common)
 
-    def send_chip(half, slot):
-        send_direct(half, div(slot, per_group), rem(slot, per_group))
-
-    def send_later(order):
-        later = per_group - AT_ONCE
-        send_direct(1, div(order, later), AT_ONCE + rem(order, later))
-
-    def transform_half(half, each_group, each_step):
+    later = per_group - AT_ONCE
+
+    def send_later(order, part):
+        send_chip(1, div(order, later), AT_ONCE + rem(order, later), part)
+
+    def transform_part(part):
         @pl.loop(0, nz)
         def _(group):
-            work.transform(group)
+            work.transform(group, (part * 4, part * 4 + 4), 4)
+
+            @pl.loop(0, 2 * per_group, step=8)
+            def _(dests):
+                for dest in range(8):
+                    dest = dests + dest
+                    work.pack_part(dest, ready.at[1, group * 2 * per_group + dest], part)
+
+            @pl.loop(0, AT_ONCE)
+            def _(step):
+                send_chip(1, group, step, part)
+
+    def transform_second():
+        @pl.loop(0, nz)
+        def _(group):
+            work.transform(group, (0, HERE), O_STRIDE)
 
             @pl.loop(0, per_group, step=4)
             def _(chips):
                 for dest in range(8):
                     dest = chips * 2 + dest
-                    work.pack(dest, ready.at[half, group * 2 * per_group + dest])
-                if each_step is not None:
-                    each_step(group * 4 + div(chips, 4))
-
-            if each_group is not None:
-                each_group(group)
-
-    def some_now(group):
-        @pl.loop(0, AT_ONCE)
-        def _(step):
-            send_direct(1, group, step)
+                    work.pack(dest, ready.at[0, group * 2 * per_group + dest])
+
+    def in_first(run):
+        send_later(run - 4 * BLOCKS, 0)
 
     def in_spread(step):
         @pl.when(rem(step, 3) == 0)
         def _():
-            send_later(div(step, 3))
+            send_later(div(step, 3), 1)
 
     def in_filter(run):
         @pl.when(rem(run, 3) == 0)
         def _():
-            send_later(9 + div(run, 3))
-
-    def in_transform(step):
-        @pl.when(step < 13)
-        def _():
-            send_later(31 + step)
+            send_later(9 + div(run, 3), 1)
 
     greeted = 1 + GREET_FIRST
     for piece, (first, count) in enumerate(PIECES):
@@ -330,9 +341,11 @@
         device_id_type=MESH,
     )
     rim_copy.start()
-    work.run_half(1)
+    work.run_half(1, (0, 4))
     fetch.wait()
-    transform_half(1, some_now, None)
+    transform_part(0)
+    work.run_half(1, (4, HERE), in_first)
+    transform_part(1)
 
     early_load.wait()
     work.spread(raw, FIRST, (0, SPLIT - 3), 4, in_spread)
@@ -345,12 +358,13 @@
 
     work.spread(rim, 1, (0, 20), 4)
     work.spread(rim, 1, (20, HALO // FRAME), 1)
-    work.run_half(0, in_filter)
-    transform_half(0, None, in_transform)
+    work.run_half(0, (0, HERE), in_filter)
+    send_later(jnp.int32(31), 1)
+    transform_second()
 
     @pl.loop(0, nz * per_group)
     def _(slot):
-        send_chip(0, slot)
+        send_chip(0, div(slot, per_group), rem(slot, per_group))
 
     for half in (1, 0):
         pltpu.make_async_copy(
@@ -364,30 +378,55 @@
 
 def correlate_kernel(segments, scale, source, vis_real, vis_imag, loaded, sem):
     channel = pl.program_id(0)
-
-    def load(c, half):
-        rows = pl.ds(pl.multiple_of(c * 2 * HERE, 2 * HERE), 2 * HERE)
+    odd = lax.rem(channel, 2)
+    tile = 2 * HERE
+
+    def second(c):
+        rows = pl.ds(pl.multiple_of(c * tile, tile), tile)
+        return pltpu.make_async_copy(source.at[0, :, rows, :], loaded.at[0, c], sem.at[0, c])
+
+    def first(pair, part):
+        rows = pl.ds(pl.multiple_of(part * PART + pair * tile, tile), tile)
+        place = pair * 2 + part
         return pltpu.make_async_copy(
-            source.at[half, :, rows, :], loaded.at[c, half], sem.at[c, half]
+            source.at[1, :, rows, :], loaded.at[1, place], sem.at[1, place]
         )
 
     @pl.when(channel == 0)
     def _():
-        for c in range(CHAN):
-            for half in range(2):
-                load(c, half).start()
-
-    for half in range(2):
-        load(channel, half).wait()
-    spectra = loaded.at[channel]
-    sources = spectra.shape[1] // segments
+        for pair in range(2):
+            for part in range(2):
+                first(pair, part).start()
+            for c in range(2):
+                second(pair * 2 + c).start()
+
+    pair = lax.div(channel, 2)
+
+    @pl.when(odd == 0)
+    def _():
+        for part in range(2):
+            first(pair, part).wait()
+
+    second(channel).wait()
+    sources = loaded.shape[2] // segments
     inputs = sources * HERE
+    upper = lax.broadcasted_iota(jnp.int32, (sources, HERE, HALF), 1) < HERE // 2
     real, imag = [], []
-    for half in range(2):
-        for segment in range(segments):
-            piece = spectra[half, segment * sources : (segment + 1) * sources].astype(jnp.float32)
-            real.append(piece[:, :HERE].reshape(inputs, HALF).astype(jnp.bfloat16))
-            imag.append(piece[:, HERE:].reshape(inputs, HALF).astype(jnp.bfloat16))
+
+    def keep(to, values):
+        to.append(values.reshape(inputs, HALF).astype(jnp.bfloat16))
+
+    for segment in range(segments):
+        here = pl.ds(segment * sources, sources)
+        piece = loaded[0, channel, here].astype(jnp.float32)
+        keep(real, piece[:, :HERE])
+        keep(imag, piece[:, HERE:])
+        parts = []
+        for part in range(2):
+            piece = loaded[1, pair * 2 + part, here].astype(jnp.float32)
+            parts.append(jnp.where(odd == 1, piece[:, HERE:], piece[:, :HERE]))
+        keep(real, jnp.where(upper, parts[0], pltpu.roll(parts[1], 4, 1)))
+        keep(imag, jnp.where(upper, pltpu.roll(parts[0], 4, 1), parts[1]))
     real = jnp.concatenate(real, axis=1)
     imag = jnp.concatenate(imag, axis=1)
 
@@ -460,8 +499,8 @@
             pl.BlockSpec((1, inputs, inputs), lambda c: (c, 0, 0)),
         ),
         scratch_shapes=[
-            pltpu.VMEM((CHAN, 2, devices, 2 * HERE, HALF), jnp.bfloat16),
-            dma((CHAN, 2)),
+            pltpu.VMEM((2, CHAN, devices, 2 * HERE, HALF), jnp.bfloat16),
+            dma((2, CHAN)),
         ],
         compiler_params=pltpu.CompilerParams(vmem_limit_bytes=60 * 2**20),
         name="correlate",

time: 80.9 us -> 78.6 us (0.972)
  Pallas kernels: 80.1 us -> 77.8 us
    pallas_call x1, Pallas kernels: 73.4 us -> 70.9 us  [per_device(): pl.pallas_call(functools.partial(exchange_kernel, dims), out_shape=jax.Sh...]
where the time goes in v1:
time: 78.6 us; the launch traced here: 78.4 us
  Pallas kernels  77.8 us (99%)
    pallas_call x1, Pallas kernels, per_device(): pl.pallas_call(functools.partial(exchange_kernel, dims), out_shape=jax.Sh...  70.9 us
    pallas_call x1, Pallas kernels, per_device(): pl.pallas_call(functools.partial(correlate_kernel, segments, 1.0 / (S_DEV...  6.95 us

profile of v1, /device:TPU:1, one launch (start us, length us, event | category | flops | bytes accessed | tf_op | source)
XLA Modules:
  0.0 78.4 jit_solution(15563198229311012079)
XLA Ops:
  0.6 70.9 %exchange.1.source = bf16[2,128,64,128]{3,2,1,0:T(8,128)(2,1)} custom-call(bf16[8,262144]{1,0:T(8,128)(2,1)} %samples.1, s32[8]{0:T(128)} %delays.1, s32[8]{0:T(128)} %flags.1, f32[16,1024]{1,0:T(8,128)} %taps.1, bf16[64,16,1024]{2,1,0:T(8,128)(2,1)} %constant.2.clone.table), custom_call_target="tpu_custom_call" | custom-call | tf_op jit(solution)/shard_map/exchange/pallas_call | solution.py:471
  71.5 6.9 %correlate.1 = (f32[4,512,512]{2,1,0:T(8,128)}, f32[4,512,512]{2,1,0:T(8,128)}) custom-call(bf16[2,128,64,128]{3,2,1,0:T(8,128)(2,1)} %exchange.1.source), custom_call_target="tpu_custom_call" | custom-call | tf_op jit(solution)/shard_map/correlate/pallas_call | solution.py:492

commit v2 on v1

--- a/solution.py
+++ b/solution.py
@@ -231,15 +231,14 @@
 
     def load(first, count, sem):
         part = pl.ds(first * FRAME, count * FRAME)
-        copy = pltpu.make_async_copy(samples.at[:, part], raw.at[:, part], sem)
-        copy.start()
-        return copy
+        return pltpu.make_async_copy(samples.at[:, part], raw.at[:, part], sem)
 
     late_loads = [
         load(first, count, load_sem.at[piece]) for piece, (first, count) in enumerate(PIECES)
     ]
+    for copy in late_loads:
+        copy.start()
     fetch = pltpu.make_async_copy(table, work.rows_table, table_sem)
-    fetch.start()
     early_load = load(0, SPLIT, load_sem.at[len(PIECES)])
     barrier = pltpu.get_barrier_semaphore()
 
@@ -318,6 +317,9 @@
     greeted = 1 + GREET_FIRST
     for piece, (first, count) in enumerate(PIECES):
         late_loads[piece].wait()
+        if piece == 1:
+            fetch.start()
+            early_load.start()
         whole = count // 4 * 4
 
         def in_late(step, begin=greeted):
@@ -394,11 +396,9 @@
 
     @pl.when(channel == 0)
     def _():
-        for pair in range(2):
-            for part in range(2):
-                first(pair, part).start()
-            for c in range(2):
-                second(pair * 2 + c).start()
+        for part in range(2):
+            first(0, part).start()
+        second(0).start()
 
     pair = lax.div(channel, 2)
 
@@ -408,6 +408,15 @@
             first(pair, part).wait()
 
     second(channel).wait()
+
+    @pl.when(channel == 0)
+    def _():
+        second(1).start()
+        for part in range(2):
+            first(1, part).start()
+        for c in range(2, CHAN):
+            second(c).start()
+
     sources = loaded.shape[2] // segments
     inputs = sources * HERE
     upper = lax.broadcasted_iota(jnp.int32, (sources, HERE, HALF), 1) < HERE // 2

time: 78.6 us -> 78.7 us (level)
  no operation moved by 1% of the time
where the time goes in v2:
time: 78.7 us; the launch traced here: 78.4 us
  Pallas kernels  77.8 us (99%)
    pallas_call x1, Pallas kernels, per_device(): pl.pallas_call(functools.partial(exchange_kernel, dims), out_shape=jax.Sh...  70.8 us
    pallas_call x1, Pallas kernels, per_device(): pl.pallas_call(functools.partial(correlate_kernel, segments, 1.0 / (S_DEV...  6.95 us

profile of v2, /device:TPU:1, one launch (start us, length us, event | category | flops | bytes accessed | tf_op | source)
XLA Modules:
  0.0 78.4 jit_solution(5622384692236834924)
XLA Ops:
  0.6 70.8 %exchange.1.source = bf16[2,128,64,128]{3,2,1,0:T(8,128)(2,1)} custom-call(bf16[8,262144]{1,0:T(8,128)(2,1)} %samples.1, s32[8]{0:T(128)} %delays.1, s32[8]{0:T(128)} %flags.1, f32[16,1024]{1,0:T(8,128)} %taps.1, bf16[64,16,1024]{2,1,0:T(8,128)(2,1)} %constant.2.clone.table), custom_call_target="tpu_custom_call" | custom-call | tf_op jit(solution)/shard_map/exchange/pallas_call | solution.py:480
  71.5 7.0 %correlate.1 = (f32[4,512,512]{2,1,0:T(8,128)}, f32[4,512,512]{2,1,0:T(8,128)}) custom-call(bf16[2,128,64,128]{3,2,1,0:T(8,128)(2,1)} %exchange.1.source), custom_call_target="tpu_custom_call" | custom-call | tf_op jit(solution)/shard_map/correlate/pallas_call | solution.py:501

commit v3 on v2

--- a/solution.py
+++ b/solution.py
@@ -444,13 +444,16 @@
 
     middle = inputs // 2
     low, high = slice(0, middle), slice(middle, inputs)
-    for rows, columns in ((low, low), (high, high), (low, high)):
-        block = product(real[rows], real[columns]) + product(imag[rows], imag[columns])
-        vis_real[0, rows, columns] = block * scale
+    for rows, columns in ((low, high), (low, low), (high, high)):
+        real_rows, imag_rows = real[rows], imag[rows]
+        real_columns, imag_columns = real[columns], imag[columns]
+        block_real = product(real_rows, real_columns) + product(imag_rows, imag_columns)
+        block_imag = product(real_rows, imag_columns) - product(imag_rows, real_columns)
+        vis_real[0, rows, columns] = block_real * scale
+        vis_imag[0, rows, columns] = block_imag * scale
         if rows != columns:
-            vis_real[0, columns, rows] = block.T * scale
-    cross = product(real, imag)
-    vis_imag[0] = (cross - cross.T) * scale
+            vis_real[0, columns, rows] = block_real.T * scale
+            vis_imag[0, columns, rows] = block_imag.T * -scale
 
 
 def per_device(samples, delays, flags, taps, *, segments, inp):

time: 78.7 us -> 79 us (level)
  no operation moved by 1% of the time
where the time goes in v3:
time: 79 us; the launch traced here: 78.7 us
  Pallas kernels  78.1 us (99%)
    pallas_call x1, Pallas kernels, per_device(): pl.pallas_call(functools.partial(exchange_kernel, dims), out_shape=jax.Sh...  70.9 us
    pallas_call x1, Pallas kernels, per_device(): pl.pallas_call(functools.partial(correlate_kernel, segments, 1.0 / (S_DEV...  7.21 us

profile of v3, /device:TPU:1, one launch (start us, length us, event | category | flops | bytes accessed | tf_op | source)
XLA Modules:
  0.0 78.7 jit_solution(15719941866251640115)
XLA Ops:
  0.6 70.9 %exchange.1.source = bf16[2,128,64,128]{3,2,1,0:T(8,128)(2,1)} custom-call(bf16[8,262144]{1,0:T(8,128)(2,1)} %samples.1, s32[8]{0:T(128)} %delays.1, s32[8]{0:T(128)} %flags.1, f32[16,1024]{1,0:T(8,128)} %taps.1, bf16[64,16,1024]{2,1,0:T(8,128)(2,1)} %constant.2.clone.table), custom_call_target="tpu_custom_call" | custom-call | tf_op jit(solution)/shard_map/exchange/pallas_call | solution.py:483
  71.5 7.2 %correlate.1 = (f32[4,512,512]{2,1,0:T(8,128)}, f32[4,512,512]{2,1,0:T(8,128)}) custom-call(bf16[2,128,64,128]{3,2,1,0:T(8,128)(2,1)} %exchange.1.source), custom_call_target="tpu_custom_call" | custom-call | tf_op jit(solution)/shard_map/correlate/pallas_call | solution.py:504

commit v4 on v2

--- a/solution.py
+++ b/solution.py
@@ -77,7 +77,7 @@
         nx, ny, nz = self.dims
         dx = rem(step, nx)
         dy = div(step, nx)
-        dz = group + 2 * nz - dx - dy
+        dz = group
         return (
             rem(self.my_x + nx + self.sign * dx, nx),
             rem(self.my_y + ny + self.sign * dy, ny),

time: 78.7 us -> 84.8 us (1.078)
  Pallas kernels: 77.8 us -> 83.9 us
    pallas_call x1, Pallas kernels: 70.8 us -> 77 us  [per_device(): pl.pallas_call(functools.partial(exchange_kernel, dims), out_shape=jax.Sh...]
where the time goes in v4:
time: 84.8 us; the launch traced here: 84.6 us
  Pallas kernels  83.9 us (99%)
    pallas_call x1, Pallas kernels, per_device(): pl.pallas_call(functools.partial(exchange_kernel, dims), out_shape=jax.Sh...  77 us
    pallas_call x1, Pallas kernels, per_device(): pl.pallas_call(functools.partial(correlate_kernel, segments, 1.0 / (S_DEV...  6.95 us

profile of v4, /device:TPU:1, one launch (start us, length us, event | category | flops | bytes accessed | tf_op | source)
XLA Modules:
  0.0 84.6 jit_solution(883879034414495259)
XLA Ops:
  0.6 77.0 %exchange.1.source = bf16[2,128,64,128]{3,2,1,0:T(8,128)(2,1)} custom-call(bf16[8,262144]{1,0:T(8,128)(2,1)} %samples.1, s32[8]{0:T(128)} %delays.1, s32[8]{0:T(128)} %flags.1, f32[16,1024]{1,0:T(8,128)} %taps.1, bf16[64,16,1024]{2,1,0:T(8,128)(2,1)} %constant.2.clone.table), custom_call_target="tpu_custom_call" | custom-call | tf_op jit(solution)/shard_map/exchange/pallas_call | solution.py:480
  77.6 7.0 %correlate.1 = (f32[4,512,512]{2,1,0:T(8,128)}, f32[4,512,512]{2,1,0:T(8,128)}) custom-call(bf16[2,128,64,128]{3,2,1,0:T(8,128)(2,1)} %exchange.1.source), custom_call_target="tpu_custom_call" | custom-call | tf_op jit(solution)/shard_map/correlate/pallas_call | solution.py:501

commit v5 on v4

--- a/solution.py
+++ b/solution.py
@@ -76,8 +76,8 @@
     def chip_of(self, group, step):
         nx, ny, nz = self.dims
         dx = rem(step, nx)
-        dy = div(step, nx)
-        dz = group
+        dy = rem(dx + div(step, nx), ny)
+        dz = group + 2 * nz - dx
         return (
             rem(self.my_x + nx + self.sign * dx, nx),
             rem(self.my_y + ny + self.sign * dy, ny),

time: 84.8 us -> 81.8 us (0.965)
  Pallas kernels: 83.9 us -> 81 us
    pallas_call x1, Pallas kernels: 77 us -> 74 us  [per_device(): pl.pallas_call(functools.partial(exchange_kernel, dims), out_shape=jax.Sh...]
where the time goes in v5:
time: 81.8 us; the launch traced here: 81.6 us
  Pallas kernels  81 us (99%)
    pallas_call x1, Pallas kernels, per_device(): pl.pallas_call(functools.partial(exchange_kernel, dims), out_shape=jax.Sh...  74 us
    pallas_call x1, Pallas kernels, per_device(): pl.pallas_call(functools.partial(correlate_kernel, segments, 1.0 / (S_DEV...  6.95 us

profile of v5, /device:TPU:1, one launch (start us, length us, event | category | flops | bytes accessed | tf_op | source)
XLA Modules:
  0.0 81.6 jit_solution(1278628796129376366)
XLA Ops:
  0.6 74.0 %exchange.1.source = bf16[2,128,64,128]{3,2,1,0:T(8,128)(2,1)} custom-call(bf16[8,262144]{1,0:T(8,128)(2,1)} %samples.1, s32[8]{0:T(128)} %delays.1, s32[8]{0:T(128)} %flags.1, f32[16,1024]{1,0:T(8,128)} %taps.1, bf16[64,16,1024]{2,1,0:T(8,128)(2,1)} %constant.2.clone.table), custom_call_target="tpu_custom_call" | custom-call | tf_op jit(solution)/shard_map/exchange/pallas_call | solution.py:480
  74.6 7.0 %correlate.1 = (f32[4,512,512]{2,1,0:T(8,128)}, f32[4,512,512]{2,1,0:T(8,128)}) custom-call(bf16[2,128,64,128]{3,2,1,0:T(8,128)(2,1)} %exchange.1.source), custom_call_target="tpu_custom_call" | custom-call | tf_op jit(solution)/shard_map/correlate/pallas_call | solution.py:501
